TPU v7x, 128 devices: a whole 4x4x4 slice. The times are simulated.
128 devices in a mesh: slab: 32 (over y_hi, x, z), dp: 4 (over y_lo, core).
Axes of the slice: x: 4, y: 4 (y_hi: 2, y_lo: 2; y = y_hi * 2 + y_lo), z: 4, core: 2. Of those that a mesh axis runs over, the one named last changes fastest.
Arguments:
- coarse_in: bfloat16 [4, 2, 64, 4, 8, 256], P('dp', None, 'slab'), may hold values from -6 to 6
- pre_up: bfloat16 [4, 2, 128, 8, 16, 128], P('dp', None, 'slab'), may hold values from -6 to 6
- pre_mid: bfloat16 [4, 2, 128, 8, 16, 128], P('dp', None, 'slab'), may hold values from -6 to 6
- grad_out: bfloat16 [4, 2, 128, 8, 16, 128], P('dp', None, 'slab'), may hold values from -6 to 6
- master: float32 [13824, 128], P(('slab', 'dp')), may hold values from -0.109375 to 0.109375
- moment: float32 [13824, 128], P(('slab', 'dp')), may hold values from -18 to 18
- second: float32 [13824, 128], P(('slab', 'dp')), may hold values from 1 to 30
Outputs:
- coarse_grad: bfloat16 [4, 2, 64, 4, 8, 256], P('dp', None, 'slab')
- new_master: float32 [13824, 128], P(('slab', 'dp'))
- new_moment: float32 [13824, 128], P(('slab', 'dp'))
- new_second: float32 [13824, 128], P(('slab', 'dp'))
All inputs are finite; a program needn't handle non-finite values.
Results may differ from a plain program's by a relative error of at most 0.0075.
Values may be sent and summed in bfloat16 or wider, within the bound.
A program may use at most 128 MiB of HBM per device.

v0:
```python
import jax
import jax.numpy as jnp
from jax import lax
from jax.sharding import PartitionSpec as P

beta_one = 0.9
beta_two = 0.999
adam_step = 10.0
learn_rate = 0.01
adam_eps = 1e-08


def padded_2(shard, sides, width):
    for axis, dim in sides:
        count, length = (lax.axis_size(axis), shard.shape[dim])
        up = [(i, (i + 1) % count) for i in range(count - 1)]
        down = [(j, i) for i, j in up]
        last = lax.slice_in_dim(shard, length - width, length, axis=dim)
        initial = lax.slice_in_dim(shard, 0, width, axis=dim)
        before = lax.ppermute(last, axis, up)
        after = lax.ppermute(initial, axis, down)
        shard = jnp.concatenate([before, shard, after], axis=dim)
    return shard


def from_behind(block, axis, distance):
    devices = range(lax.axis_size(axis))
    route = [(i - distance, i) for i in devices if i - distance in devices]
    return lax.ppermute(block, axis, route)


def correlate(padded, weight):
    samples_here, depth_ext, height, breadth, in_width = padded.shape
    inner_depth = depth_ext - 2
    lateral = jnp.pad(padded, ((0, 0), (0, 0), (1, 1), (1, 1), (0, 0)))
    running = None
    for depth_tap in range(3):
        for row_tap in range(3):
            columns = jnp.concatenate(
                [
                    lateral[
                        :,
                        depth_tap : depth_tap + inner_depth,
                        row_tap : row_tap + height,
                        col_tap : col_tap + breadth,
                        :,
                    ]
                    for col_tap in range(3)
                ],
                axis=-1,
            )
            row_start = (depth_tap * 3 + row_tap) * 3 * in_width
            product_term = jnp.dot(
                columns.reshape(-1, 3 * in_width),
                weight[row_start : row_start + 3 * in_width],
                preferred_element_type=jnp.float32,
            )
            running = product_term if running is None else running + product_term
    return running.reshape(samples_here, inner_depth, height, breadth, weight.shape[1])


def filter_grad(padded, grads):
    samples_here, depth_ext, height, breadth, in_width = padded.shape
    inner_depth = depth_ext - 2
    lateral = jnp.pad(padded, ((0, 0), (0, 0), (1, 1), (1, 1), (0, 0)))
    flat_grads = grads.reshape(-1, grads.shape[-1])
    blocks = []
    for depth_tap in range(3):
        for row_tap in range(3):
            columns = jnp.concatenate(
                [
                    lateral[
                        :,
                        depth_tap : depth_tap + inner_depth,
                        row_tap : row_tap + height,
                        col_tap : col_tap + breadth,
                        :,
                    ]
                    for col_tap in range(3)
                ],
                axis=-1,
            )
            blocks.append(
                lax.dot_general(
                    columns.reshape(-1, 3 * in_width),
                    flat_grads,
                    (((0,), (0,)), ((), ())),
                    preferred_element_type=jnp.float32,
                )
            )
    return jnp.concatenate(blocks, axis=0)


def flipped(weight, in_width):
    out_width = weight.shape[1]
    shaped = weight.reshape(3, 3, 3, in_width, out_width)[::-1, ::-1, ::-1]
    return shaped.transpose(0, 1, 2, 4, 3).reshape(27 * out_width, in_width)


def upconv_back(grad_pad, coarse, weight):
    lateral = jnp.pad(grad_pad, ((0, 0), (0, 0), (1, 0), (1, 0), (0, 0)))
    samples_here, coarse_depth, coarse_rows, coarse_cols, coarse_width = coarse.shape
    fine_width = weight.shape[1]
    slices = []
    for depth_tap in range(3):
        for row_tap in range(3):
            for col_tap in range(3):
                slices.append(
                    lateral[
                        :,
                        depth_tap : depth_tap + 2 * coarse_depth : 2,
                        row_tap : row_tap + 2 * coarse_rows : 2,
                        col_tap : col_tap + 2 * coarse_cols : 2,
                        :,
                    ]
                )
    gathered = jnp.concatenate(slices, axis=-1).reshape(-1, 27 * fine_width)
    turned = (
        weight.reshape(27, coarse_width, fine_width)
        .transpose(0, 2, 1)
        .reshape(27 * fine_width, coarse_width)
    )
    coarse_grad = jnp.dot(gathered, turned, preferred_element_type=jnp.float32).reshape(
        coarse.shape
    )
    filter_part = lax.dot_general(
        coarse.reshape(-1, coarse_width),
        gathered,
        (((0,), (0,)), ((), ())),
        preferred_element_type=jnp.float32,
    )
    filter_part = (
        filter_part.reshape(coarse_width, 27, fine_width)
        .transpose(1, 0, 2)
        .reshape(27 * coarse_width, fine_width)
    )
    return (coarse_grad, filter_part)


def body(coarse_in, pre_up, pre_mid, grad_out, master, moment, second):
    channels = pre_up.shape[-1]
    group_size = pre_up.shape[1]
    shards = lax.all_gather(master.astype(jnp.bfloat16), ("slab", "dp"), axis=0, tiled=True)
    w_one = shards[: 27 * channels]
    w_two = shards[27 * channels : 54 * channels]
    w_up = shards[54 * channels :]
    flip_one = flipped(w_one, channels)
    flip_two = flipped(w_two, channels)
    up_in = pre_up.reshape((-1,) + pre_up.shape[2:])
    mid_in = pre_mid.reshape((-1,) + pre_mid.shape[2:])
    out_in = grad_out.reshape((-1,) + grad_out.shape[2:])
    rim_block = padded_2(jnp.stack([jax.nn.relu(mid_in), out_in]), (("slab", 2),), 1)
    mid_act = rim_block[0]
    out_pad = rim_block[1]
    grad_two = filter_grad(mid_act, out_in)
    back_mid = correlate(out_pad, flip_two)
    mid_grad = jnp.where(mid_in > 0, back_mid, 0.0).astype(jnp.bfloat16)
    inner_rims = padded_2(jnp.stack([jax.nn.relu(up_in), mid_grad]), (("slab", 2),), 1)
    up_act = inner_rims[0]
    mid_grad_pad = inner_rims[1]
    grad_one = filter_grad(up_act, mid_grad)
    back_up = correlate(mid_grad_pad, flip_one)
    up_grad = jnp.where(up_in > 0, back_up, 0.0).astype(jnp.bfloat16)
    previous = from_behind(up_grad[:, -1:], "slab", 1)
    grad_pad = jnp.concatenate([previous, up_grad], axis=1)
    coarse_here = coarse_in.reshape((-1,) + coarse_in.shape[2:])
    coarse_grad, grad_up = upconv_back(grad_pad, coarse_here, w_up)
    coarse_grad = coarse_grad.astype(jnp.bfloat16).reshape(coarse_in.shape)
    partial_value = jnp.concatenate([grad_one, grad_two, grad_up], axis=0)
    totals = lax.psum(partial_value, ("slab", "dp"))
    own_rows = master.shape[0]
    summed = lax.dynamic_slice_in_dim(
        totals, lax.axis_index(("slab", "dp")) * own_rows, own_rows, 0
    )
    mean_grad = summed / float(group_size * lax.axis_size("dp"))
    new_moment = beta_one * moment + (1.0 - beta_one) * mean_grad
    new_second = beta_two * second + (1.0 - beta_two) * mean_grad * mean_grad
    corrected = new_moment / (1.0 - beta_one**adam_step)
    scaled = jnp.sqrt(new_second / (1.0 - beta_two**adam_step)) + adam_eps
    new_master = master - learn_rate * corrected / scaled
    return (coarse_grad, new_master, new_moment, new_second)


def solution(mesh):
    return jax.shard_map(
        body,
        mesh=mesh,
        in_specs=(
            P("dp", None, "slab", None, None, None),
            P("dp", None, "slab", None, None, None),
            P("dp", None, "slab", None, None, None),
            P("dp", None, "slab", None, None, None),
            P(("slab", "dp"), None),
            P(("slab", "dp"), None),
            P(("slab", "dp"), None),
        ),
        out_specs=(
            P("dp", None, "slab", None, None, None),
            P(("slab", "dp"), None),
            P(("slab", "dp"), None),
            P(("slab", "dp"), None),
        ),
        check_vma=False,
    )
```

profile of v0, /device:TPU:1, one launch (start us, length us, event | category | flops | bytes accessed | tf_op | source)
XLA Modules:
  0.0 458.4 jit_solution(18084580664319161008)
XLA Ops:
  7.2 1.5 convert_bitcast_fusion
  10.7 1.3 collective-permute-start.1
  12.0 5.0 %collective-permute-start = (bf16[2,2,1,8,16,128]{5,4,3,2,1,0:T(8,128)(2,1)S(1)}, bf16[2,2,1,8,16,128]{5,4,3,2,1,0:T(8,128)(2,1)S(1)}, u32[]{:S(2)}, u32[]{:S(2)}) collective-permute-start(bf16[2,2,1,8,16,128]{5,4,3,2,1,0:T(8,128)(2,1)S(1)} %get-tuple-element.15), channel_id=1, source_target_pairs={{0,4},{4,8},{8,12},{12,16},{16,20},{20,24},{24,28},{28,32},{32,36}... | collective-permute-start | bytes 393224 | tf_op jit(solution)/shard_map/ppermute | solution.py:20
  32.9 1.4 pad_maximum_fusion.3
  34.3 1.5 pad_maximum_fusion.6
  35.8 1.4 pad_maximum_fusion.22
  37.2 1.4 pad_maximum_fusion.25
  38.6 172.9 %all-gather.3.cloned.1.call-done = bf16[128,108,128]{2,1,0:T(8,128)(2,1)} async-done(((bf16[1,108,128]{2,1,0:T(8,128)(2,1)}), bf16[128,108,128]{2,1,0:T(8,128)(2,1)}) %all-gather.3.cloned.1.call-update) | async-done | bytes 3538960 | tf_op jit(solution)/shard_map/all_gather | solution.py:143
  211.5 1.6 fusion.90
  213.3 1.4 copy.17
  214.7 1.6 fusion.79
  222.0 1.3 collective-permute-start.3
  223.3 4.6 %collective-permute-start.2 = (bf16[2,2,1,8,16,128]{5,4,3,2,1,0:T(8,128)(2,1)}, bf16[2,2,1,8,16,128]{5,4,3,2,1,0:T(8,128)(2,1)}, u32[]{:S(2)}, u32[]{:S(2)}) collective-permute-start(bf16[2,2,1,8,16,128]{5,4,3,2,1,0:T(8,128)(2,1)} %get-tuple-element.13), channel_id=1, source_target_pairs={{0,4},{4,8},{8,12},{12,16},{16,20},{20,24},{24,28},{28,32},{32,36}... | collective-permute-start | bytes 393224 | tf_op jit(solution)/shard_map/ppermute | solution.py:20
  228.2 1.4 copy.18
  239.3 3.8 collective-permute-start.4
  251.7 2.9 copy-done.2
  269.2 2.4 fusion.91
  271.6 5.2 %copy.20 = f32[27,256,128]{2,1,0:T(8,128)} copy(f32[27,256,128]{1,2,0:T(8,128)} %bitcast.181) | data formatting | bytes 7077888 | tf_op jit(solution)/shard_map/transpose | solution.py:134
  276.8 4.1 constant_dynamic-update-slice_fusion.27
  280.9 1.5 slice-done
  282.4 1.4 reshape.171
  283.8 2.6 copy.19
  287.5 162.5 %all-reduce.7.cloned.1.call-done = f32[13824,128]{1,0:T(8,128)} async-done(((f32[13824,128]{1,0:T(8,128)}), f32[13824,128]{1,0:T(8,128)}) %all-reduce.7.cloned.1.call-update) | async-done | bytes 7077904 | tf_op jit(solution)/shard_map/psum | solution.py:170
  450.0 1.5 divide_subtract_fusion
  (198 shorter events, 56.9 us)
Async XLA Ops:
  7.2 262.0 %copy-start = (bf16[1,2,2,4,8,256]{5,4,3,2,1,0:T(8,128)(2,1)S(1)}, bf16[1,2,2,4,8,256]{5,4,3,2,1,0:T(8,128)(2,1)}, u32[]{:S(2)}) copy-start(bf16[1,2,2,4,8,256]{5,4,3,2,1,0:T(8,128)(2,1)} %param.7) | copy-start | bytes 196612
  7.2 12.0 %copy-start.1 = (bf16[1,2,4,8,16,128]{5,4,3,2,1,0:T(8,128)(2,1)S(1)}, bf16[1,2,4,8,16,128]{5,4,3,2,1,0:T(8,128)(2,1)}, u32[]{:S(2)}) copy-start(bf16[1,2,4,8,16,128]{5,4,3,2,1,0:T(8,128)(2,1)} %param.10) | copy-start | bytes 786436
  7.2 9.8 %copy-start.23 = (bf16[1,2,4,8,16,128]{5,4,3,2,1,0:T(8,128)(2,1)S(1)}, bf16[1,2,4,8,16,128]{5,4,3,2,1,0:T(8,128)(2,1)}, u32[]{:S(2)}) copy-start(bf16[1,2,4,8,16,128]{5,4,3,2,1,0:T(8,128)(2,1)} %param.8) | copy-start | bytes 786436
  7.2 204.3 %all-gather.3.cloned.1.call-start = ((), (), s32[]{:S(2)}) async-start(), calls=%async_computation.1 | async-start | bytes 3698688 | tf_op jit(solution)/shard_map/all_gather | solution.py:143
  8.8 441.2 %all-reduce.7.cloned.1.call-start = ((), (), s32[]{:S(2)}) async-start(), calls=%async_computation | async-start | bytes 14155776 | tf_op jit(solution)/shard_map/psum | solution.py:170
  10.7 7.6 %collective-permute-start.1 = (bf16[2,2,1,8,16,128]{5,4,3,2,1,0:T(8,128)(2,1)S(1)}, bf16[2,2,1,8,16,128]{5,4,3,2,1,0:T(8,128)(2,1)S(1)}, u32[]{:S(2)}, u32[]{:S(2)}) collective-permute-start(bf16[2,2,1,8,16,128]{5,4,3,2,1,0:T(8,128)(2,1)S(1)} %get-tuple-element.16), channel_id=1, source_target_pairs={{4,0},{8,4},{12,8},{16,12},{20,16},{24,20},{28,24},{32,28},{36,32}... | collective-permute-start | bytes 393224 | tf_op jit(solution)/shard_map/ppermute | solution.py:21
  12.0 7.1 %collective-permute-start = (bf16[2,2,1,8,16,128]{5,4,3,2,1,0:T(8,128)(2,1)S(1)}, bf16[2,2,1,8,16,128]{5,4,3,2,1,0:T(8,128)(2,1)S(1)}, u32[]{:S(2)}, u32[]{:S(2)}) collective-permute-start(bf16[2,2,1,8,16,128]{5,4,3,2,1,0:T(8,128)(2,1)S(1)} %get-tuple-element.15), channel_id=1, source_target_pairs={{0,4},{4,8},{8,12},{12,16},{16,20},{20,24},{24,28},{28,32},{32,36}... | collective-permute-start | bytes 393224 | tf_op jit(solution)/shard_map/ppermute | solution.py:20
  214.7 1.6 copy-start.15
  214.7 2.0 copy-start.18
  222.0 7.7 %collective-permute-start.3 = (bf16[2,2,1,8,16,128]{5,4,3,2,1,0:T(8,128)(2,1)}, bf16[2,2,1,8,16,128]{5,4,3,2,1,0:T(8,128)(2,1)}, u32[]{:S(2)}, u32[]{:S(2)}) collective-permute-start(bf16[2,2,1,8,16,128]{5,4,3,2,1,0:T(8,128)(2,1)} %get-tuple-element.14), channel_id=1, source_target_pairs={{4,0},{8,4},{12,8},{16,12},{20,16},{24,20},{28,24},{32,28},{36,32}... | collective-permute-start | bytes 393224 | tf_op jit(solution)/shard_map/ppermute | solution.py:21
  223.3 6.4 %collective-permute-start.2 = (bf16[2,2,1,8,16,128]{5,4,3,2,1,0:T(8,128)(2,1)}, bf16[2,2,1,8,16,128]{5,4,3,2,1,0:T(8,128)(2,1)}, u32[]{:S(2)}, u32[]{:S(2)}) collective-permute-start(bf16[2,2,1,8,16,128]{5,4,3,2,1,0:T(8,128)(2,1)} %get-tuple-element.13), channel_id=1, source_target_pairs={{0,4},{4,8},{8,12},{12,16},{16,20},{20,24},{24,28},{28,32},{32,36}... | collective-permute-start | bytes 393224 | tf_op jit(solution)/shard_map/ppermute | solution.py:20
  228.2 1.5 copy-start.22
  239.3 15.4 %collective-permute-start.4 = (bf16[2,1,8,16,128]{4,3,2,1,0:T(8,128)(2,1)S(1)}, bf16[2,1,8,16,128]{4,3,2,1,0:T(8,128)(2,1)S(1)}, u32[]{:S(2)}, u32[]{:S(2)}) collective-permute-start(bf16[2,1,8,16,128]{4,3,2,1,0:T(8,128)(2,1)S(1)} %slice.703), channel_id=1, source_target_pairs={{0,4},{4,8},{8,12},{12,16},{16,20},{20,24},{24,28},{28,32},{32,36}... | collective-permute-start | bytes 196616 | tf_op jit(solution)/shard_map/ppermute | solution.py:29
  246.6 1.6 copy-start.7
  247.0 1.6 copy-start.11
  248.1 1.3 copy-start.5
  248.6 1.3 copy-start.12
  249.0 1.3 copy-start.10
  249.5 1.3 copy-start.3
  251.7 3.0 copy-start.2
  280.9 1.5 slice-start
  286.4 163.6 %copy-start.25 = (f32[108,128]{1,0:T(8,128)S(1)}, f32[108,128]{1,0:T(8,128)}, u32[]{:S(2)}) copy-start(f32[108,128]{1,0:T(8,128)} %param.11) | copy-start | bytes 165892
  286.5 163.5 %copy-start.26 = (f32[108,128]{1,0:T(8,128)S(1)}, f32[108,128]{1,0:T(8,128)}, u32[]{:S(2)}) copy-start(f32[108,128]{1,0:T(8,128)} %param.12) | copy-start | bytes 165892
  286.5 163.5 %copy-start.27 = (f32[108,128]{1,0:T(8,128)S(1)}, f32[108,128]{1,0:T(8,128)}, u32[]{:S(2)}) copy-start(f32[108,128]{1,0:T(8,128)} %param.13) | copy-start | bytes 165892
  (12 other events, 13.8 us)
Sparse Core Ops, SparseCore 0:
  10.3 201.1 all-gather.2
  281.1 168.8 all-reduce.6
where the time goes:
time: 459 us; the launch traced here: 458 us
  waiting for transfers between devices  337 us (73%)
  local copies, waits for them, and re-layouts  46.5 us (10%)
  other arithmetic  24.8 us (5%)
  matrix products  18.9 us (4%)
  starting transfers between devices  16.1 us (4%)
  between operations  15.3 us (3%)
    all_gather x1, waiting for transfers between devices, body(): lax.all_gather(master.astype(jnp.bfloat16), ('slab', 'dp'), axis=0, tiled...  173 us
    psum x1, waiting for transfers between devices, body(): totals = lax.psum(partial_value, ('slab', 'dp'))  162 us
    slice x27, local copies, waits for them, and re-layouts, upconv_back(): lateral[:, depth_tap:depth_tap + 2 * coarse_depth:2, row_tap:row_tap + 2...  13.7 us
    ppermute x2, starting transfers between devices, padded_2(): before = lax.ppermute(last, axis, up)  9.65 us
  transfers between devices with their start and end apart: 7, of which 4 were waited for; matrix products, arithmetic and copies ran while one was open for 8% of the time, Pallas kernels for 0%

commit v1 on v0

--- a/solution.py
+++ b/solution.py
@@ -8,6 +8,13 @@
 adam_step = 10.0
 learn_rate = 0.01
 adam_eps = 1e-08
+
+
+def swapped_in(x, axis, dim):
+    peers = lax.axis_size(axis)
+    tiles = jnp.stack([x for _ in range(peers)])
+    tiles = lax.all_to_all(tiles, axis, split_axis=0, concat_axis=0)
+    return jnp.concatenate(tiles, axis=dim)
 
 
 def padded_2(shard, sides, width):
@@ -140,7 +147,7 @@
 def body(coarse_in, pre_up, pre_mid, grad_out, master, moment, second):
     channels = pre_up.shape[-1]
     group_size = pre_up.shape[1]
-    shards = lax.all_gather(master.astype(jnp.bfloat16), ("slab", "dp"), axis=0, tiled=True)
+    shards = swapped_in(master.astype(jnp.bfloat16), ("slab", "dp"), 0)
     w_one = shards[: 27 * channels]
     w_two = shards[27 * channels : 54 * channels]
     w_up = shards[54 * channels :]

time: 459 us -> 336 us (0.73)
  waiting for transfers between devices: 337 us -> 203 us
  starting transfers between devices: 16.1 us -> 27 us
    all_gather x1 -> x0, waiting for transfers between devices: 173 us -> none  [body(): lax.all_gather(master.astype(jnp.bfloat16), ('slab', 'dp'), axis=0, tiled...]
    ppermute x2, waiting for transfers between devices: 0.54 us -> 40.1 us  [padded_2(): after = lax.ppermute(initial, axis, down)]
    all_to_all x0 -> x1, starting transfers between devices: none -> 11.9 us  [swapped_in(): tiles = lax.all_to_all(tiles, axis, split_axis=0, concat_axis=0)]
  transfers between devices with their start and end apart: 7 -> 7, of which waited for: 4 -> 2; matrix products, arithmetic and copies ran while one was open for 8% -> 11% of each run, Pallas kernels for 0% -> 0%
where the time goes in v1:
time: 336 us; the launch traced here: 335 us
  waiting for transfers between devices  203 us (60%)
  local copies, waits for them, and re-layouts  48.9 us (15%)
  starting transfers between devices  27 us (8%)
  other arithmetic  22.2 us (7%)
  matrix products  18.9 us (6%)
  between operations  15.3 us (5%)
    psum x1, waiting for transfers between devices, body(): totals = lax.psum(partial_value, ('slab', 'dp'))  163 us
    ppermute x2, waiting for transfers between devices, padded_2(): after = lax.ppermute(initial, axis, down)  40.1 us
    slice x27, local copies, waits for them, and re-layouts, upconv_back(): lateral[:, depth_tap:depth_tap + 2 * coarse_depth:2, row_tap:row_tap + 2...  13.7 us
    all_to_all x1, starting transfers between devices, swapped_in(): tiles = lax.all_to_all(tiles, axis, split_axis=0, concat_axis=0)  11.9 us
    concatenate x16, other arithmetic, correlate(): jnp.concatenate([lateral[:, depth_tap:depth_tap + inner_depth, row_tap:ro...  8.79 us
    ppermute x2, starting transfers between devices, padded_2(): before = lax.ppermute(last, axis, up)  8.68 us
    concatenate x7, other arithmetic, filter_grad(): jnp.concatenate([lateral[:, depth_tap:depth_tap + inner_depth, row_tap:ro...  7.92 us
    dot_general x18, matrix products, correlate(): jnp.dot(columns.reshape(-1, 3 * in_width), weight[row_start:row_start + 3...  7.8 us
  transfers between devices with their start and end apart: 7, of which 2 were waited for; matrix products, arithmetic and copies ran while one was open for 11% of the time, Pallas kernels for 0%

profile of v1, /device:TPU:1, one launch (start us, length us, event | category | flops | bytes accessed | tf_op | source)
XLA Modules:
  0.0 335.4 jit_solution(6067333080668229953)
XLA Ops:
  8.0 2.3 stack.7
  10.3 11.9 %all-to-all-start = ((bf16[128,108,128]{2,1,0:T(8,128)(2,1)}), bf16[128,108,128]{2,1,0:T(8,128)(2,1)}, u32[]{:S(2)}, u32[]{:S(2)}) async-start(bf16[128,108,128]{2,1,0:T(8,128)(2,1)} %stack.7), calls=%async_computation | async-start | bytes 7340032 | tf_op jit(solution)/shard_map/all_to_all | solution.py:16
  22.3 1.3 collective-permute-start.1
  23.6 4.0 %collective-permute-start = (bf16[2,2,1,8,16,128]{5,4,3,2,1,0:T(8,128)(2,1)S(1)}, bf16[2,2,1,8,16,128]{5,4,3,2,1,0:T(8,128)(2,1)S(1)}, u32[]{:S(2)}, u32[]{:S(2)}) collective-permute-start(bf16[2,2,1,8,16,128]{5,4,3,2,1,0:T(8,128)(2,1)S(1)} %get-tuple-element.15), channel_id=1, source_target_pairs={{0,4},{4,8},{8,12},{12,16},{16,20},{20,24},{24,28},{28,32},{32,36}... | collective-permute-start | bytes 393224 | tf_op jit(solution)/shard_map/ppermute | solution.py:27
  28.5 40.1 %collective-permute-done.1 = bf16[2,2,1,8,16,128]{5,4,3,2,1,0:T(8,128)(2,1)S(1)} collective-permute-done((bf16[2,2,1,8,16,128]{5,4,3,2,1,0:T(8,128)(2,1)S(1)}, bf16[2,2,1,8,16,128]{5,4,3,2,1,0:T(8,128)(2,1)S(1)}, u32[]{:S(2)}, u32[]{:S(2)}) %collective-permute-start.1) | collective-permute-done | bytes 131104 | tf_op jit(solution)/shard_map/ppermute | solution.py:28
  82.3 1.4 pad_maximum_fusion.3
  83.7 1.4 pad_maximum_fusion.6
  85.1 1.4 pad_maximum_fusion.22
  86.5 1.5 pad_maximum_fusion.25
  88.0 1.6 fusion.90
  89.8 1.4 copy.12
  91.2 1.6 fusion.79
  99.7 4.6 %collective-permute-start.2 = (bf16[2,2,1,8,16,128]{5,4,3,2,1,0:T(8,128)(2,1)}, bf16[2,2,1,8,16,128]{5,4,3,2,1,0:T(8,128)(2,1)}, u32[]{:S(2)}, u32[]{:S(2)}) collective-permute-start(bf16[2,2,1,8,16,128]{5,4,3,2,1,0:T(8,128)(2,1)} %get-tuple-element.13), channel_id=1, source_target_pairs={{0,4},{4,8},{8,12},{12,16},{16,20},{20,24},{24,28},{28,32},{32,36}... | collective-permute-start | bytes 393224 | tf_op jit(solution)/shard_map/ppermute | solution.py:27
  104.6 1.4 copy.13
  115.7 3.8 %collective-permute-start.4 = (bf16[2,1,8,16,128]{4,3,2,1,0:T(8,128)(2,1)S(1)}, bf16[2,1,8,16,128]{4,3,2,1,0:T(8,128)(2,1)S(1)}, u32[]{:S(2)}, u32[]{:S(2)}) collective-permute-start(bf16[2,1,8,16,128]{4,3,2,1,0:T(8,128)(2,1)S(1)} %slice.703), channel_id=1, source_target_pairs={{0,4},{4,8},{8,12},{12,16},{16,20},{20,24},{24,28},{28,32},{32,36}... | collective-permute-start | bytes 196616 | tf_op jit(solution)/shard_map/ppermute | solution.py:36
  128.1 2.9 copy-done.2
  145.6 2.4 fusion.91
  148.0 5.2 %copy.15 = f32[27,256,128]{2,1,0:T(8,128)} copy(f32[27,256,128]{1,2,0:T(8,128)} %bitcast.179) | data formatting | bytes 7077888 | tf_op jit(solution)/shard_map/transpose | solution.py:141
  153.2 4.1 %constant_dynamic-update-slice_fusion.27 = f32[13824,128]{1,0:T(8,128)} fusion(f32[13824,128]{1,0:T(8,128)} %copy-done.2, f32[6912,128]{1,0:T(8,128)} %bitcast.178), kind=kLoop, calls=%fused_computation.285 | loop fusion | bytes 7077888 | tf_op jit(solution)/shard_map/concatenate | solution.py:176
  157.3 1.6 slice.704
  159.0 1.4 reshape.180
  160.4 2.6 copy.14
  164.1 162.9 %all-reduce.7.cloned.1.call-done = f32[13824,128]{1,0:T(8,128)} async-done(((f32[13824,128]{1,0:T(8,128)}), f32[13824,128]{1,0:T(8,128)}) %all-reduce.7.cloned.1.call-update) | async-done | bytes 7077904 | tf_op jit(solution)/shard_map/psum | solution.py:177
  327.0 1.5 divide_subtract_fusion
  (197 shorter events, 55.6 us)
Async XLA Ops:
  7.2 138.4 %copy-start = (bf16[1,2,2,4,8,256]{5,4,3,2,1,0:T(8,128)(2,1)S(1)}, bf16[1,2,2,4,8,256]{5,4,3,2,1,0:T(8,128)(2,1)}, u32[]{:S(2)}) copy-start(bf16[1,2,2,4,8,256]{5,4,3,2,1,0:T(8,128)(2,1)} %param.7) | copy-start | bytes 196612
  10.3 12.0 %copy-start.20 = (bf16[1,2,4,8,16,128]{5,4,3,2,1,0:T(8,128)(2,1)S(1)}, bf16[1,2,4,8,16,128]{5,4,3,2,1,0:T(8,128)(2,1)}, u32[]{:S(2)}) copy-start(bf16[1,2,4,8,16,128]{5,4,3,2,1,0:T(8,128)(2,1)} %param.9) | copy-start | bytes 786436
  10.3 12.0 %copy-start.1 = (bf16[1,2,4,8,16,128]{5,4,3,2,1,0:T(8,128)(2,1)S(1)}, bf16[1,2,4,8,16,128]{5,4,3,2,1,0:T(8,128)(2,1)}, u32[]{:S(2)}) copy-start(bf16[1,2,4,8,16,128]{5,4,3,2,1,0:T(8,128)(2,1)} %param.10) | copy-start | bytes 786436
  10.3 17.4 %copy-start.23 = (bf16[1,2,4,8,16,128]{5,4,3,2,1,0:T(8,128)(2,1)S(1)}, bf16[1,2,4,8,16,128]{5,4,3,2,1,0:T(8,128)(2,1)}, u32[]{:S(2)}) copy-start(bf16[1,2,4,8,16,128]{5,4,3,2,1,0:T(8,128)(2,1)} %param.8) | copy-start | bytes 786436
  10.3 77.7 %all-to-all-start = ((bf16[128,108,128]{2,1,0:T(8,128)(2,1)}), bf16[128,108,128]{2,1,0:T(8,128)(2,1)}, u32[]{:S(2)}, u32[]{:S(2)}) async-start(bf16[128,108,128]{2,1,0:T(8,128)(2,1)} %stack.7), calls=%async_computation | async-start | bytes 7340032 | tf_op jit(solution)/shard_map/all_to_all | solution.py:16
  22.2 304.8 %all-reduce.7.cloned.1.call-start = ((), (), s32[]{:S(2)}) async-start(), calls=%async_computation.1 | async-start | bytes 14155776 | tf_op jit(solution)/shard_map/psum | solution.py:177
  22.3 46.3 %collective-permute-start.1 = (bf16[2,2,1,8,16,128]{5,4,3,2,1,0:T(8,128)(2,1)S(1)}, bf16[2,2,1,8,16,128]{5,4,3,2,1,0:T(8,128)(2,1)S(1)}, u32[]{:S(2)}, u32[]{:S(2)}) collective-permute-start(bf16[2,2,1,8,16,128]{5,4,3,2,1,0:T(8,128)(2,1)S(1)} %get-tuple-element.16), channel_id=1, source_target_pairs={{4,0},{8,4},{12,8},{16,12},{20,16},{24,20},{28,24},{32,28},{36,32}... | collective-permute-start | bytes 393224 | tf_op jit(solution)/shard_map/ppermute | solution.py:28
  23.6 45.0 %collective-permute-start = (bf16[2,2,1,8,16,128]{5,4,3,2,1,0:T(8,128)(2,1)S(1)}, bf16[2,2,1,8,16,128]{5,4,3,2,1,0:T(8,128)(2,1)S(1)}, u32[]{:S(2)}, u32[]{:S(2)}) collective-permute-start(bf16[2,2,1,8,16,128]{5,4,3,2,1,0:T(8,128)(2,1)S(1)} %get-tuple-element.15), channel_id=1, source_target_pairs={{0,4},{4,8},{8,12},{12,16},{16,20},{20,24},{24,28},{28,32},{32,36}... | collective-permute-start | bytes 393224 | tf_op jit(solution)/shard_map/ppermute | solution.py:27
  91.2 1.6 copy-start.15
  91.2 2.0 copy-start.18
  98.4 7.7 %collective-permute-start.3 = (bf16[2,2,1,8,16,128]{5,4,3,2,1,0:T(8,128)(2,1)}, bf16[2,2,1,8,16,128]{5,4,3,2,1,0:T(8,128)(2,1)}, u32[]{:S(2)}, u32[]{:S(2)}) collective-permute-start(bf16[2,2,1,8,16,128]{5,4,3,2,1,0:T(8,128)(2,1)} %get-tuple-element.14), channel_id=1, source_target_pairs={{4,0},{8,4},{12,8},{16,12},{20,16},{24,20},{28,24},{32,28},{36,32}... | collective-permute-start | bytes 393224 | tf_op jit(solution)/shard_map/ppermute | solution.py:28
  99.7 6.4 %collective-permute-start.2 = (bf16[2,2,1,8,16,128]{5,4,3,2,1,0:T(8,128)(2,1)}, bf16[2,2,1,8,16,128]{5,4,3,2,1,0:T(8,128)(2,1)}, u32[]{:S(2)}, u32[]{:S(2)}) collective-permute-start(bf16[2,2,1,8,16,128]{5,4,3,2,1,0:T(8,128)(2,1)} %get-tuple-element.13), channel_id=1, source_target_pairs={{0,4},{4,8},{8,12},{12,16},{16,20},{20,24},{24,28},{28,32},{32,36}... | collective-permute-start | bytes 393224 | tf_op jit(solution)/shard_map/ppermute | solution.py:27
  104.6 1.5 copy-start.22
  115.7 15.4 %collective-permute-start.4 = (bf16[2,1,8,16,128]{4,3,2,1,0:T(8,128)(2,1)S(1)}, bf16[2,1,8,16,128]{4,3,2,1,0:T(8,128)(2,1)S(1)}, u32[]{:S(2)}, u32[]{:S(2)}) collective-permute-start(bf16[2,1,8,16,128]{4,3,2,1,0:T(8,128)(2,1)S(1)} %slice.703), channel_id=1, source_target_pairs={{0,4},{4,8},{8,12},{12,16},{16,20},{20,24},{24,28},{28,32},{32,36}... | collective-permute-start | bytes 196616 | tf_op jit(solution)/shard_map/ppermute | solution.py:36
  123.0 1.6 copy-start.7
  123.4 1.6 copy-start.11
  124.6 1.3 copy-start.5
  125.0 1.3 copy-start.12
  125.4 1.3 copy-start.10
  125.9 1.3 copy-start.3
  128.1 3.0 copy-start.2
  163.0 164.0 %copy-start.25 = (f32[108,128]{1,0:T(8,128)S(1)}, f32[108,128]{1,0:T(8,128)}, u32[]{:S(2)}) copy-start(f32[108,128]{1,0:T(8,128)} %param.11) | copy-start | bytes 165892
  163.0 164.0 %copy-start.26 = (f32[108,128]{1,0:T(8,128)S(1)}, f32[108,128]{1,0:T(8,128)}, u32[]{:S(2)}) copy-start(f32[108,128]{1,0:T(8,128)} %param.12) | copy-start | bytes 165892
  163.0 164.0 %copy-start.27 = (f32[108,128]{1,0:T(8,128)S(1)}, f32[108,128]{1,0:T(8,128)}, u32[]{:S(2)}) copy-start(f32[108,128]{1,0:T(8,128)} %param.13) | copy-start | bytes 165892
  (11 other events, 12.8 us)
Sparse Core Ops, SparseCore 0:
  157.5 169.5 all-reduce.6
